TPU v7x, 512 devices: a whole 4x4x16 slice. The times are simulated.
512 devices in a mesh: row: 16 (over z_lo, x), col: 32 (over z_hi, y, core).
Axes of the slice: x: 4, y: 4, z: 16 (z_hi: 4, z_lo: 4; z = z_hi * 4 + z_lo), core: 2. Of those that a mesh axis runs over, the one named last changes fastest.
Arguments:
- inputs: bfloat16 [512, 12288], P('col', 'row'), may hold values from -6 to 6
- w_in: bfloat16 [12288, 24576], P('row', 'col'), may hold values from -0.0546875 to 0.0546875
- w_out: bfloat16 [24576, 12288], P('col', 'row'), may hold values from -0.0390625 to 0.0390625
- cotangent: bfloat16 [512, 12288], P('col', 'row'), may hold values from -6 to 6
Outputs:
- output: bfloat16 [512, 12288], P('col', 'row')
- grad_inputs: bfloat16 [512, 12288], P('col', 'row')
- grad_w_in: bfloat16 [12288, 24576], P('row', 'col')
- grad_w_out: bfloat16 [24576, 12288], P('col', 'row')
All inputs are finite; a program needn't handle non-finite values.
Results may differ from a plain program's by a relative error of at most 0.034.
Values may be sent and summed in bfloat16 or wider, within the bound.
No kernel may reach another device: no remote copies, remote signals or barrier semaphores. Data moves between devices by JAX's collectives and lax.ppermute only.
A program may use at most 64 MiB of HBM per device.

v0:
```python
import jax
import jax.numpy as jnp
from jax import lax
from jax.sharding import PartitionSpec as P


def gelu_tanh(values):
    return jax.nn.gelu(values, approximate=True)


def gelu_grad(hidden, upstream):
    pullback = jax.vjp(gelu_tanh, hidden)[1]
    return pullback(upstream)[0]


def plain_product(left, right):
    return jnp.dot(left, right, preferred_element_type=jnp.float32)


def transposed_product(left, right):
    return lax.dot_general(
        left, right, (((1,), (1,)), ((), ())), preferred_element_type=jnp.float32
    )


def per_device(inputs, w_in, w_out, cotangent):
    input_all = lax.all_gather(inputs, "col", axis=0, tiled=True)
    cotangent_all = lax.all_gather(cotangent, "col", axis=0, tiled=True)
    picked = input_all
    hidden = lax.psum_scatter(
        plain_product(picked, w_in).astype(jnp.bfloat16), "row", scatter_dimension=0, tiled=True
    ).astype(jnp.float32)
    active_share = gelu_tanh(hidden).astype(jnp.bfloat16)
    active_all = lax.all_gather(active_share, "row", axis=0, tiled=True)
    picked = cotangent_all
    grad_active = lax.psum_scatter(
        transposed_product(picked, w_out).astype(jnp.bfloat16),
        "row",
        scatter_dimension=0,
        tiled=True,
    ).astype(jnp.float32)
    grad_hidden = gelu_grad(hidden, grad_active).astype(jnp.bfloat16)
    grad_hidden_all = lax.all_gather(grad_hidden, "row", axis=0, tiled=True)
    picked = active_all
    output = lax.psum_scatter(
        plain_product(picked, w_out).astype(jnp.bfloat16), "col", scatter_dimension=0, tiled=True
    )
    picked = grad_hidden_all
    grad_inputs = lax.psum_scatter(
        transposed_product(picked, w_in).astype(jnp.bfloat16),
        "col",
        scatter_dimension=0,
        tiled=True,
    )
    grad_w_in = lax.dot_general(
        input_all, grad_hidden_all, (((0,), (0,)), ((), ())), preferred_element_type=jnp.float32
    ).astype(jnp.bfloat16)
    grad_w_out = lax.dot_general(
        active_all, cotangent_all, (((0,), (0,)), ((), ())), preferred_element_type=jnp.float32
    ).astype(jnp.bfloat16)
    return (output, grad_inputs, grad_w_in, grad_w_out)


def solution(mesh):
    return jax.shard_map(
        per_device,
        mesh=mesh,
        in_specs=(P("col", "row"), P("row", "col"), P("col", "row"), P("col", "row")),
        out_specs=(P("col", "row"), P("col", "row"), P("row", "col"), P("col", "row")),
        check_vma=False,
    )
```

profile of v0, /device:TPU:4, one launch (start us, length us, event | category | flops | bytes accessed | tf_op | source)
XLA Modules:
  0.0 520.9 jit_solution(15499417743574480613)
XLA Ops:
  7.2 0.0 copy-start
  7.2 0.0 reduce-scatter.9.cloned.1.call-start
  7.2 62.7 %all_gather.14 = bf16[512,768]{1,0:T(8,128)(2,1)S(1)} all-gather(bf16[16,768]{1,0:T(8,128)(2,1)} %param.7), channel_id=1, replica_groups=mesh['row'=16,'col'=32] {'col'}, dimensions={0}, use_global_device_ids=true | all-gather | bytes 811008 | tf_op jit(solution)/shard_map/all_gather | solution.py:28
  69.9 0.0 copy-start.4
  69.9 3.0 convolution_convert_fusion.3
  72.9 0.0 reduce-scatter.9.cloned.1.call-update
  72.9 0.0 reduce-scatter.5.cloned.1.call-start
  72.9 0.0 copy-done.4
  72.9 51.9 %all_gather.12 = bf16[512,768]{1,0:T(8,128)(2,1)S(1)} all-gather(bf16[16,768]{1,0:T(8,128)(2,1)S(1)} %copy-done.4), channel_id=1, replica_groups=mesh['row'=16,'col'=32] {'col'}, dimensions={0}, use_global_device_ids=true | all-gather | bytes 811008 | tf_op jit(solution)/shard_map/all_gather | solution.py:27
  124.9 0.9 copy-done.1
  125.7 0.0 copy-done
  125.7 1.7 convolution_convert_fusion.5
  127.4 0.0 reduce-scatter.5.cloned.1.call-update
  127.4 0.0 reduce-scatter.11.cloned.1.call-start
  127.5 24.5 %reduce-scatter.9.cloned.1.call-done = bf16[32,768]{1,0:T(8,128)(2,1)} async-done(((bf16[512,768]{1,0:T(8,128)(2,1)}), bf16[32,768]{1,0:T(8,128)(2,1)}) %reduce-scatter.9.cloned.1.call-update) | async-done | bytes 49168 | tf_op jit(solution)/shard_map/reduce_scatter | solution.py:36
  151.9 89.0 %reduce-scatter.5.cloned.1.call-done = bf16[32,768]{1,0:T(8,128)(2,1)} async-done(((bf16[512,768]{1,0:T(8,128)(2,1)}), bf16[32,768]{1,0:T(8,128)(2,1)}) %reduce-scatter.5.cloned.1.call-update) | async-done | bytes 49168 | tf_op jit(solution)/shard_map/reduce_scatter | solution.py:30
  241.0 0.9 fusion.4
  241.9 42.8 %all_gather.15 = bf16[512,768]{1,0:T(8,128)(2,1)S(1)} all-gather(bf16[32,768]{1,0:T(8,128)(2,1)S(1)} %get-tuple-element.8), channel_id=1, replica_groups=mesh['row'=16,'col'=32] {'row'}, dimensions={0}, use_global_device_ids=true | all-gather | bytes 835584 | tf_op jit(solution)/shard_map/all_gather | solution.py:43
  284.7 0.9 copy-done.2
  285.6 1.7 convolution_convert_fusion.2
  287.3 0.0 reduce-scatter.11.cloned.1.call-update
  287.3 0.0 reduce-scatter.7.cloned.1.call-start
  287.4 41.2 %all_gather.13 = bf16[512,768]{1,0:T(8,128)(2,1)S(1)} all-gather(bf16[32,768]{1,0:T(8,128)(2,1)S(1)} %get-tuple-element.9), channel_id=1, replica_groups=mesh['row'=16,'col'=32] {'row'}, dimensions={0}, use_global_device_ids=true | all-gather | bytes 835584 | tf_op jit(solution)/shard_map/all_gather | solution.py:34
  328.5 0.9 copy-done.3
  329.4 0.0 copy-done.5
  329.4 1.7 convolution_convert_fusion.4
  331.1 0.0 reduce-scatter.7.cloned.1.call-update
  331.1 2.2 fusion
  333.3 1.5 copy.8
  334.7 3.0 convolution_convert_fusion
  337.7 65.0 %reduce-scatter.11.cloned.1.call-done = bf16[16,768]{1,0:T(8,128)(2,1)} async-done(((bf16[512,768]{1,0:T(8,128)(2,1)}), bf16[16,768]{1,0:T(8,128)(2,1)}) %reduce-scatter.11.cloned.1.call-update) | async-done | bytes 24592 | tf_op jit(solution)/shard_map/reduce_scatter | solution.py:49
  402.7 111.6 %reduce-scatter.7.cloned.1.call-done = bf16[16,768]{1,0:T(8,128)(2,1)} async-done(((bf16[512,768]{1,0:T(8,128)(2,1)}), bf16[16,768]{1,0:T(8,128)(2,1)}) %reduce-scatter.7.cloned.1.call-update) | async-done | bytes 24592 | tf_op jit(solution)/shard_map/reduce_scatter | solution.py:45
  (4 shorter events, 0.0 us)
Async XLA Ops:
  7.2 118.6 %copy-start = (bf16[768,768]{1,0:T(8,128)(2,1)S(1)}, bf16[768,768]{1,0:T(8,128)(2,1)}, u32[]{:S(2)}) copy-start(bf16[768,768]{1,0:T(8,128)(2,1)} %param.5) | copy-start | bytes 3538948
  7.2 144.8 %reduce-scatter.9.cloned.1.call-start = ((), (), s32[]{:S(2)}) async-start(), calls=%async_computation.6 | async-start | bytes 835584 | tf_op jit(solution)/shard_map/reduce_scatter | solution.py:36
  69.9 3.0 copy-start.4
  72.9 168.1 %reduce-scatter.5.cloned.1.call-start = ((), (), s32[]{:S(2)}) async-start(), calls=%async_computation.4 | async-start | bytes 835584 | tf_op jit(solution)/shard_map/reduce_scatter | solution.py:30
  124.9 0.9 copy-start.1
  127.4 275.3 %reduce-scatter.11.cloned.1.call-start = ((), (), s32[]{:S(2)}) async-start(), calls=%async_computation.7 | async-start | bytes 811008 | tf_op jit(solution)/shard_map/reduce_scatter | solution.py:49
  284.7 0.9 copy-start.2
  287.3 42.1 %copy-start.5 = (bf16[768,768]{1,0:T(8,128)(2,1)S(1)}, bf16[768,768]{1,0:T(8,128)(2,1)}, u32[]{:S(2)}) copy-start(bf16[768,768]{1,0:T(8,128)(2,1)} %param.6) | copy-start | bytes 3538948
  287.3 227.1 %reduce-scatter.7.cloned.1.call-start = ((), (), s32[]{:S(2)}) async-start(), calls=%async_computation.5 | async-start | bytes 811008 | tf_op jit(solution)/shard_map/reduce_scatter | solution.py:45
  328.5 0.9 copy-start.3
Sparse Core Ops, SparseCore 0:
  73.0 78.8 reduce-scatter.8
  155.5 85.3 reduce-scatter.4
  287.4 115.2 reduce-scatter.10
  407.5 106.8 reduce-scatter.6
where the time goes:
time: 521 us
  waiting for transfers between devices  290 us (56%)
  blocking collectives  199 us (38%)
  between operations  13.8 us (3%)
  matrix products  13.1 us (3%)
    reduce_scatter x1, waiting for transfers between devices, per_device(): lax.psum_scatter(plain_product(picked, w_out).astype(jnp.bfloat16), 'col'...  112 us
    reduce_scatter x1, waiting for transfers between devices, per_device(): lax.psum_scatter(plain_product(picked, w_in).astype(jnp.bfloat16), 'row',...  89 us
    reduce_scatter x1, waiting for transfers between devices, per_device(): lax.psum_scatter(transposed_product(picked, w_in).astype(jnp.bfloat16), '...  65 us
    all_gather x1, blocking collectives, per_device(): cotangent_all = lax.all_gather(cotangent, 'col', axis=0, tiled=True)  62.7 us
    all_gather x1, blocking collectives, per_device(): input_all = lax.all_gather(inputs, 'col', axis=0, tiled=True)  51.9 us
    all_gather x1, blocking collectives, per_device(): grad_hidden_all = lax.all_gather(grad_hidden, 'row', axis=0, tiled=True)  42.8 us
    all_gather x1, blocking collectives, per_device(): active_all = lax.all_gather(active_share, 'row', axis=0, tiled=True)  41.2 us
    reduce_scatter x1, waiting for transfers between devices, per_device(): lax.psum_scatter(transposed_product(picked, w_out).astype(jnp.bfloat16),...  24.5 us
  transfers between devices with their start and end apart: 4, of which 4 were waited for; matrix products, arithmetic and copies ran while one was open for 2% of the time, Pallas kernels for 0%

commit v1 on v0

v1 whole, which is shorter than its diff:
```python
import jax
import jax.numpy as jnp
from jax import lax
from jax.sharding import Mesh, PartitionSpec as P

F32 = jnp.float32
BF16 = jnp.bfloat16


def gelu_tanh(values):
    return jax.nn.gelu(values, approximate=True)


def product(left, right, dims):
    return lax.dot_general(left, right, (dims, ((), ())), preferred_element_type=F32).astype(BF16)


def exchange(parts, axis):
    return lax.all_to_all(parts, axis, 0, 0)


def gather(share, axis, size):
    return exchange(jnp.broadcast_to(share[None], (size, *share.shape)), axis)


def summed(parts):
    return jnp.sum(parts.astype(F32), axis=0)


def swap_cores(values):
    return lax.ppermute(values, "core", [(0, 1), (1, 0)])


def per_device(inputs, w_in, w_out, cotangent):
    rows, width = inputs.shape
    units = w_in.shape[1]
    size = {name: lax.axis_size(name) for name in ("z_lo", "x", "z_hi", "y", "core")}

    share = jnp.concatenate([inputs, cotangent], axis=1)
    own = gather(gather(share, "z_hi", size["z_hi"]), "y", size["y"])
    own = own.reshape(-1, 2 * width)
    other = swap_cores(own)
    half = own.shape[0]
    tokens = jnp.concatenate([own, other], axis=0)
    input_all, cotangent_all = tokens[:, :width], tokens[:, width:]

    terms = jnp.concatenate(
        [product(input_all, w_in, ((1,), (0,))), product(cotangent_all, w_out, ((1,), (1,)))], axis=1
    )
    parts = exchange(terms.reshape(size["x"], -1, 2 * units), "x")
    parts = summed(parts).astype(BF16).reshape(size["z_lo"], -1, 2 * units)
    both = summed(exchange(parts, "z_lo"))
    hidden, grad_active = both[:, :units], both[:, units:]
    active, pullback = jax.vjp(gelu_tanh, hidden)
    share = jnp.concatenate([active.astype(BF16), pullback(grad_active)[0].astype(BF16)], axis=1)
    both = gather(gather(share, "z_lo", size["z_lo"]), "x", size["x"]).reshape(2 * half, 2 * units)
    active_all, grad_hidden_all = both[:, :units], both[:, units:]

    def layer_terms(rows):
        return jnp.concatenate(
            [
                product(active_all[rows], w_out, ((1,), (0,))),
                product(grad_hidden_all[rows], w_in, ((1,), (1,))),
            ],
            axis=1,
        )

    arriving = swap_cores(layer_terms(slice(half, None)))
    kept = layer_terms(slice(0, half))
    grad_w_in = product(input_all, grad_hidden_all, ((0,), (0,)))
    grad_w_out = product(active_all, cotangent_all, ((0,), (0,)))
    parts = (kept.astype(F32) + arriving.astype(F32)).astype(BF16)
    parts = exchange(parts.reshape(size["y"], -1, 2 * width), "y")
    parts = summed(parts).astype(BF16).reshape(size["z_hi"], -1, 2 * width)
    both = summed(exchange(parts, "z_hi")).astype(BF16)
    return both[:, :width], both[:, width:], grad_w_in, grad_w_out


def solution(mesh):
    fine = Mesh(mesh.devices.reshape(4, 4, 4, 4, 2), ("z_lo", "x", "z_hi", "y", "core"))
    row, col = ("z_lo", "x"), ("z_hi", "y", "core")
    return jax.shard_map(
        per_device,
        mesh=fine,
        in_specs=(P(col, row), P(row, col), P(col, row), P(col, row)),
        out_specs=(P(col, row), P(col, row), P(row, col), P(col, row)),
        check_vma=False,
    )
```

time: 521 us -> 173 us (0.33)
  the two profiles are of different devices: /device:TPU:4 before, /device:TPU:2 now
where the time goes in v1:
time: 173 us
  blocking collectives  136 us (79%)
  waiting for transfers between devices  15.6 us (9%)
  matrix products  8.44 us (5%)
  starting transfers between devices  7.46 us (4%)
  other arithmetic  2.44 us (1%)
    all_to_all x7, blocking collectives, exchange(): return lax.all_to_all(parts, axis, 0, 0)  136 us
    all_to_all x1, waiting for transfers between devices, exchange(): return lax.all_to_all(parts, axis, 0, 0)  12.1 us
    dot_general x8, matrix products, product(): lax.dot_general(left, right, (dims, ((), ())), preferred_element_type=F32)  8.44 us
    ppermute x2, starting transfers between devices, swap_cores(): return lax.ppermute(values, 'core', [(0, 1), (1, 0)])  3.83 us
    all_to_all x1, starting transfers between devices, exchange(): return lax.all_to_all(parts, axis, 0, 0)  3.63 us
    ppermute x2, waiting for transfers between devices, swap_cores(): return lax.ppermute(values, 'core', [(0, 1), (1, 0)])  3.51 us
  transfers between devices with their start and end apart: 3, of which 3 were waited for; matrix products, arithmetic and copies ran while one was open for 3% of the time, Pallas kernels for 0%

profile of v1, /device:TPU:2, one launch (start us, length us, event | category | flops | bytes accessed | tf_op | source)
XLA Modules:
  0.0 172.6 jit_solution(1370371533679725966)
XLA Ops:
  0.6 0.9 pad_maximum_fusion.6
  1.5 32.0 %all_to_all.40 = bf16[4,16,1536]{2,1,0:T(8,128)(2,1)S(1)} all-to-all(bf16[4,16,1536]{2,1,0:T(8,128)(2,1)S(1)} %broadcast_in_dim.8), channel_id=1, replica_groups=mesh['z_lo'=4,'x'=4,'z_hi'=4,'y'=4,'core'=2] {'z_hi'}, dimensions={0} | all-to-all | bytes 393216 | tf_op jit(solution)/shard_map/all_to_all | solution.py:19
  33.5 0.1 broadcast_in_dim.9
  33.6 13.8 %all_to_all.41 = bf16[4,4,16,1536]{3,2,1,0:T(8,128)(2,1)S(1)} all-to-all(bf16[4,4,16,1536]{3,2,1,0:T(8,128)(2,1)S(1)} %broadcast_in_dim.9), channel_id=1, replica_groups=mesh['z_lo'=4,'x'=4,'z_hi'=4,'y'=4,'core'=2] {'y'}, dimensions={0} | all-to-all | bytes 1572864 | tf_op jit(solution)/shard_map/all_to_all | solution.py:19
  47.3 1.9 %collective-permute-start = (bf16[256,1536]{1,0:T(8,128)(2,1)S(1)}, bf16[256,1536]{1,0:T(8,128)(2,1)S(1)}, u32[]{:S(2)}, u32[]{:S(2)}) collective-permute-start(bf16[256,1536]{1,0:T(8,128)(2,1)S(1)} %bitcast.22), channel_id=1, source_target_pairs={{0,1},{1,0},{2,3},{3,2},{4,5},{5,4},{6,7},{7,6},{8,9},{9,8},{10,11... | collective-permute-start | bytes 2359304 | tf_op jit(solution)/shard_map/ppermute | solution.py:31
  49.2 2.3 %collective-permute-done = bf16[256,1536]{1,0:T(8,128)(2,1)S(1)} collective-permute-done((bf16[256,1536]{1,0:T(8,128)(2,1)S(1)}, bf16[256,1536]{1,0:T(8,128)(2,1)S(1)}, u32[]{:S(2)}, u32[]{:S(2)}) %collective-permute-start) | collective-permute-done | bytes 786464 | tf_op jit(solution)/shard_map/ppermute | solution.py:31
  51.5 0.8 convolution_convert_fusion.2
  52.4 0.8 convolution_convert_fusion.3
  53.2 0.1 pad_maximum_fusion
  53.3 24.2 %all_to_all.42 = bf16[4,128,1536]{2,1,0:T(8,128)(2,1)S(1)} all-to-all(bf16[4,128,1536]{2,1,0:T(8,128)(2,1)S(1)} %bitcast.12), channel_id=1, replica_groups=mesh['z_lo'=4,'x'=4,'z_hi'=4,'y'=4,'core'=2] {'x'}, dimensions={0} | all-to-all | bytes 3145728 | tf_op jit(solution)/shard_map/all_to_all | solution.py:19
  77.5 0.3 reduce_sum.45
  77.7 16.0 %all_to_all.43 = bf16[4,32,1536]{2,1,0:T(8,128)(2,1)S(1)} all-to-all(bf16[4,32,1536]{2,1,0:T(8,128)(2,1)S(1)} %bitcast.20), channel_id=1, replica_groups=mesh['z_lo'=4,'x'=4,'z_hi'=4,'y'=4,'core'=2] {'z_lo'}, dimensions={0} | all-to-all | bytes 786432 | tf_op jit(solution)/shard_map/all_to_all | solution.py:19
  93.7 0.1 multiply_convert_fusion
  93.9 13.1 %all_to_all.44 = bf16[4,32,1536]{2,1,0:T(8,128)(2,1)S(1)} all-to-all(bf16[4,32,1536]{2,1,0:T(8,128)(2,1)S(1)} %broadcast_in_dim.10), channel_id=1, replica_groups=mesh['z_lo'=4,'x'=4,'z_hi'=4,'y'=4,'core'=2] {'z_lo'}, dimensions={0} | all-to-all | bytes 786432 | tf_op jit(solution)/shard_map/all_to_all | solution.py:19
  107.0 0.1 broadcast_in_dim.11
  107.1 21.8 %all_to_all.45 = bf16[4,4,32,1536]{3,2,1,0:T(8,128)(2,1)S(1)} all-to-all(bf16[4,4,32,1536]{3,2,1,0:T(8,128)(2,1)S(1)} %broadcast_in_dim.11), channel_id=1, replica_groups=mesh['z_lo'=4,'x'=4,'z_hi'=4,'y'=4,'core'=2] {'x'}, dimensions={0} | all-to-all | bytes 3145728 | tf_op jit(solution)/shard_map/all_to_all | solution.py:19
  129.0 0.5 convolution_convert_fusion.4
  129.5 0.8 copy-done.4
  130.2 0.5 convolution_convert_fusion.5
  130.7 0.1 pad_maximum_fusion.2
  130.8 1.9 %collective-permute-start.1 = (bf16[256,1536]{1,0:T(8,128)(2,1)S(1)}, bf16[256,1536]{1,0:T(8,128)(2,1)S(1)}, u32[]{:S(2)}, u32[]{:S(2)}) collective-permute-start(bf16[256,1536]{1,0:T(8,128)(2,1)S(1)} %pad_maximum_fusion.2), channel_id=1, source_target_pairs={{0,1},{1,0},{2,3},{3,2},{4,5},{5,4},{6,7},{7,6},{8,9},{9,8},{10,11... | collective-permute-start | bytes 2359304 | tf_op jit(solution)/shard_map/ppermute | solution.py:31
  132.7 0.5 convolution_convert_fusion.6
  133.2 0.5 convolution_convert_fusion.7
  133.7 1.3 collective-permute-done.1
  135.0 0.2 add_convert_fusion
  135.1 15.3 %all_to_all.46 = bf16[4,64,1536]{2,1,0:T(8,128)(2,1)S(1)} all-to-all(bf16[4,64,1536]{2,1,0:T(8,128)(2,1)S(1)} %bitcast.13), channel_id=1, replica_groups=mesh['z_lo'=4,'x'=4,'z_hi'=4,'y'=4,'core'=2] {'y'}, dimensions={0} | all-to-all | bytes 1572864 | tf_op jit(solution)/shard_map/all_to_all | solution.py:19
  150.4 0.8 reduce_sum.47
  151.2 3.6 %all-to-all-start.7 = ((bf16[4,16,1536]{2,1,0:T(8,128)(2,1)}), bf16[4,16,1536]{2,1,0:T(8,128)(2,1)S(1)}, u32[]{:S(2)}, u32[]{:S(2)}) async-start(bf16[4,16,1536]{2,1,0:T(8,128)(2,1)} %bitcast.21), calls=%async_computation.7 | async-start | bytes 393216 | tf_op jit(solution)/shard_map/all_to_all | solution.py:19
  154.9 3.1 %convolution_convert_fusion = bf16[768,768]{1,0:T(8,128)(2,1)} fusion(bf16[512,1536]{1,0:T(8,128)(2,1)S(1)} %bitcast.18, bf16[256,1536]{1,0:T(8,128)(2,1)} %copy-done.5, bf16[256,1536]{1,0:T(8,128)(2,1)} %bitcast.25), kind=kOutput, calls=%fused_computation.4 | convolution fusion | flops 606142464 | bytes 3538944 | tf_op jit(solution)/shard_map/dot_general | solution.py:15
  157.9 1.8 %convolution_convert_fusion.1 = bf16[768,768]{1,0:T(8,128)(2,1)} fusion(bf16[512,1536]{1,0:T(8,128)(2,1)S(1)} %bitcast.19, bf16[256,1536]{1,0:T(8,128)(2,1)S(1)} %bitcast.26, bf16[256,1536]{1,0:T(8,128)(2,1)S(1)} %copy-done.6), kind=kOutput, calls=%fused_computation.5 | convolution fusion | flops 606142464 | bytes 3538944 | tf_op jit(solution)/shard_map/dot_general | solution.py:15
  159.8 12.1 %all-to-all-done.7 = bf16[4,16,1536]{2,1,0:T(8,128)(2,1)S(1)} async-done(((bf16[4,16,1536]{2,1,0:T(8,128)(2,1)}), bf16[4,16,1536]{2,1,0:T(8,128)(2,1)S(1)}, u32[]{:S(2)}, u32[]{:S(2)}) %all-to-all-start.7) | async-done | bytes 196640 | tf_op jit(solution)/shard_map/all_to_all | solution.py:19
  171.9 0.6 fusion.18
  (18 shorter events, 0.2 us)
Async XLA Ops:
  0.6 51.7 %copy-start = (bf16[768,768]{1,0:T(8,128)(2,1)S(1)}, bf16[768,768]{1,0:T(8,128)(2,1)}, u32[]{:S(2)}) copy-start(bf16[768,768]{1,0:T(8,128)(2,1)} %param.5) | copy-start | bytes 3538948
  1.5 50.0 %copy-start.3 = (bf16[768,768]{1,0:T(8,128)(2,1)S(1)}, bf16[768,768]{1,0:T(8,128)(2,1)}, u32[]{:S(2)}) copy-start(bf16[768,768]{1,0:T(8,128)(2,1)} %param.6) | copy-start | bytes 3538948
  47.3 5.0 %copy-start.1 = (bf16[4,4,16,1536]{3,2,1,0:T(8,128)(2,1)}, bf16[4,4,16,1536]{3,2,1,0:T(8,128)(2,1)S(1)}, u32[]{:S(2)}) copy-start(bf16[4,4,16,1536]{3,2,1,0:T(8,128)(2,1)S(1)} %all_to_all.41) | copy-start | bytes 2359300
  47.3 4.2 %collective-permute-start = (bf16[256,1536]{1,0:T(8,128)(2,1)S(1)}, bf16[256,1536]{1,0:T(8,128)(2,1)S(1)}, u32[]{:S(2)}, u32[]{:S(2)}) collective-permute-start(bf16[256,1536]{1,0:T(8,128)(2,1)S(1)} %bitcast.22), channel_id=1, source_target_pairs={{0,1},{1,0},{2,3},{3,2},{4,5},{5,4},{6,7},{7,6},{8,9},{9,8},{10,11... | collective-permute-start | bytes 2359304 | tf_op jit(solution)/shard_map/ppermute | solution.py:31
  51.5 0.9 copy-start.5
  129.0 1.3 copy-start.4
  130.8 4.2 %collective-permute-start.1 = (bf16[256,1536]{1,0:T(8,128)(2,1)S(1)}, bf16[256,1536]{1,0:T(8,128)(2,1)S(1)}, u32[]{:S(2)}, u32[]{:S(2)}) collective-permute-start(bf16[256,1536]{1,0:T(8,128)(2,1)S(1)} %pad_maximum_fusion.2), channel_id=1, source_target_pairs={{0,1},{1,0},{2,3},{3,2},{4,5},{5,4},{6,7},{7,6},{8,9},{9,8},{10,11... | collective-permute-start | bytes 2359304 | tf_op jit(solution)/shard_map/ppermute | solution.py:31
  151.2 20.7 %all-to-all-start.7 = ((bf16[4,16,1536]{2,1,0:T(8,128)(2,1)}), bf16[4,16,1536]{2,1,0:T(8,128)(2,1)S(1)}, u32[]{:S(2)}, u32[]{:S(2)}) async-start(bf16[4,16,1536]{2,1,0:T(8,128)(2,1)} %bitcast.21), calls=%async_computation.7 | async-start | bytes 393216 | tf_op jit(solution)/shard_map/all_to_all | solution.py:19
  154.9 3.1 %copy-start.2 = (bf16[4,4,16,1536]{3,2,1,0:T(8,128)(2,1)S(1)}, bf16[4,4,16,1536]{3,2,1,0:T(8,128)(2,1)}, u32[]{:S(2)}) copy-start(bf16[4,4,16,1536]{3,2,1,0:T(8,128)(2,1)} %copy-done.1) | copy-start | bytes 2359300
  154.9 3.1 %copy-start.6 = (bf16[256,1536]{1,0:T(8,128)(2,1)S(1)}, bf16[256,1536]{1,0:T(8,128)(2,1)}, u32[]{:S(2)}) copy-start(bf16[256,1536]{1,0:T(8,128)(2,1)} %copy-done.5) | copy-start | bytes 2359300

commit v2 on v1

--- a/solution.py
+++ b/solution.py
@@ -27,19 +27,20 @@
     return jnp.sum(parts.astype(F32), axis=0)
 
 
-def swap_cores(values):
-    return lax.ppermute(values, "core", [(0, 1), (1, 0)])
+def swapped(values, axis):
+    return lax.ppermute(values, axis, [(0, 1), (1, 0)])
 
 
 def per_device(inputs, w_in, w_out, cotangent):
     rows, width = inputs.shape
     units = w_in.shape[1]
-    size = {name: lax.axis_size(name) for name in ("z_lo", "x", "z_hi", "y", "core")}
+    size = {name: lax.axis_size(name) for name in ("z_pair", "x", "z_hi", "y")}
+    plane = size["z_pair"] * size["x"]
 
     share = jnp.concatenate([inputs, cotangent], axis=1)
     own = gather(gather(share, "z_hi", size["z_hi"]), "y", size["y"])
     own = own.reshape(-1, 2 * width)
-    other = swap_cores(own)
+    other = swapped(own, "core")
     half = own.shape[0]
     tokens = jnp.concatenate([own, other], axis=0)
     input_all, cotangent_all = tokens[:, :width], tokens[:, width:]
@@ -47,13 +48,13 @@
     terms = jnp.concatenate(
         [product(input_all, w_in, ((1,), (0,))), product(cotangent_all, w_out, ((1,), (1,)))], axis=1
     )
-    parts = exchange(terms.reshape(size["x"], -1, 2 * units), "x")
-    parts = summed(parts).astype(BF16).reshape(size["z_lo"], -1, 2 * units)
-    both = summed(exchange(parts, "z_lo"))
+    parts = exchange(terms.reshape(plane, -1, 2 * units), ("z_pair", "x"))
+    part = summed(parts).astype(BF16)
+    both = part.astype(F32) + swapped(part, "z_half").astype(F32)
     hidden, grad_active = both[:, :units], both[:, units:]
     active, pullback = jax.vjp(gelu_tanh, hidden)
     share = jnp.concatenate([active.astype(BF16), pullback(grad_active)[0].astype(BF16)], axis=1)
-    both = gather(gather(share, "z_lo", size["z_lo"]), "x", size["x"]).reshape(2 * half, 2 * units)
+    both = gather(share, ("z_pair", "x"), plane).reshape(2 * half, 2 * units)
     active_all, grad_hidden_all = both[:, :units], both[:, units:]
 
     def layer_terms(rows):
@@ -65,7 +66,7 @@
             axis=1,
         )
 
-    arriving = swap_cores(layer_terms(slice(half, None)))
+    arriving = swapped(layer_terms(slice(half, None)), "core")
     kept = layer_terms(slice(0, half))
     grad_w_in = product(input_all, grad_hidden_all, ((0,), (0,)))
     grad_w_out = product(active_all, cotangent_all, ((0,), (0,)))
@@ -77,8 +78,9 @@
 
 
 def solution(mesh):
-    fine = Mesh(mesh.devices.reshape(4, 4, 4, 4, 2), ("z_lo", "x", "z_hi", "y", "core"))
-    row, col = ("z_lo", "x"), ("z_hi", "y", "core")
+    names = ("z_half", "z_pair", "x", "z_hi", "y", "core")
+    fine = Mesh(mesh.devices.reshape(2, 2, 4, 4, 4, 2), names)
+    row, col = names[:3], names[3:]
     return jax.shard_map(
         per_device,
         mesh=fine,

time: 173 us -> 162 us (0.936)
  the two profiles are of different devices: /device:TPU:2 before, /device:TPU:64 now
where the time goes in v2:
time: 162 us; the launch traced here: 161 us
  blocking collectives  114 us (70%)
  waiting for transfers between devices  22.6 us (14%)
  starting transfers between devices  11.3 us (7%)
  matrix products  8.44 us (5%)
  other arithmetic  2.47 us (2%)
  local copies, waits for them, and re-layouts  1.68 us (1%)
    all_to_all x5, blocking collectives, exchange(): return lax.all_to_all(parts, axis, 0, 0)  114 us
    all_to_all x1, waiting for transfers between devices, exchange(): return lax.all_to_all(parts, axis, 0, 0)  12.3 us
    ppermute x3, waiting for transfers between devices, swapped(): return lax.ppermute(values, axis, [(0, 1), (1, 0)])  10.4 us
    dot_general x8, matrix products, product(): lax.dot_general(left, right, (dims, ((), ())), preferred_element_type=F32)  8.44 us
    ppermute x3, starting transfers between devices, swapped(): return lax.ppermute(values, axis, [(0, 1), (1, 0)])  7.66 us
    all_to_all x1, starting transfers between devices, exchange(): return lax.all_to_all(parts, axis, 0, 0)  3.62 us
  transfers between devices with their start and end apart: 4, of which 4 were waited for; matrix products, arithmetic and copies ran while one was open for 4% of the time, Pallas kernels for 0%

profile of v2, /device:TPU:64, one launch (start us, length us, event | category | flops | bytes accessed | tf_op | source)
XLA Modules:
  0.0 161.4 jit_solution(16139832185953362153)
XLA Ops:
  0.6 0.9 pad_maximum_fusion.6
  1.5 32.0 %all_to_all.30 = bf16[4,16,1536]{2,1,0:T(8,128)(2,1)S(1)} all-to-all(bf16[4,16,1536]{2,1,0:T(8,128)(2,1)S(1)} %broadcast_in_dim.6), channel_id=1, replica_groups=mesh['z_half'=2,'z_pair'=2,'x'=4,'z_hi'=4,'y'=4,'core'=2] {'z_hi'}, dimensions={0} | all-to-all | bytes 393216 | tf_op jit(solution)/shard_map/all_to_all | solution.py:19
  33.6 0.1 broadcast_in_dim.7
  33.6 14.8 %all_to_all.31 = bf16[4,4,16,1536]{3,2,1,0:T(8,128)(2,1)S(1)} all-to-all(bf16[4,4,16,1536]{3,2,1,0:T(8,128)(2,1)S(1)} %broadcast_in_dim.7), channel_id=1, replica_groups=mesh['z_half'=2,'z_pair'=2,'x'=4,'z_hi'=4,'y'=4,'core'=2] {'y'}, dimensions={0} | all-to-all | bytes 1572864 | tf_op jit(solution)/shard_map/all_to_all | solution.py:19
  48.4 1.9 %collective-permute-start = (bf16[256,1536]{1,0:T(8,128)(2,1)S(1)}, bf16[256,1536]{1,0:T(8,128)(2,1)S(1)}, u32[]{:S(2)}, u32[]{:S(2)}) collective-permute-start(bf16[256,1536]{1,0:T(8,128)(2,1)S(1)} %bitcast.20), channel_id=1, source_target_pairs={{0,1},{1,0},{2,3},{3,2},{4,5},{5,4},{6,7},{7,6},{8,9},{9,8},{10,11... | collective-permute-start | bytes 2359304 | tf_op jit(solution)/shard_map/ppermute | solution.py:31
  50.3 2.3 %collective-permute-done = bf16[256,1536]{1,0:T(8,128)(2,1)S(1)} collective-permute-done((bf16[256,1536]{1,0:T(8,128)(2,1)S(1)}, bf16[256,1536]{1,0:T(8,128)(2,1)S(1)}, u32[]{:S(2)}, u32[]{:S(2)}) %collective-permute-start) | collective-permute-done | bytes 786464 | tf_op jit(solution)/shard_map/ppermute | solution.py:31
  52.6 0.8 convolution_convert_fusion.2
  53.4 0.1 copy-done.5
  53.5 0.8 convolution_convert_fusion.3
  54.3 0.1 pad_maximum_fusion
  54.4 25.7 %all_to_all.32 = bf16[8,64,1536]{2,1,0:T(8,128)(2,1)S(1)} all-to-all(bf16[8,64,1536]{2,1,0:T(8,128)(2,1)S(1)} %bitcast.11), channel_id=1, replica_groups=mesh['z_half'=2,'z_pair'=2,'x'=4,'z_hi'=4,'y'=4,'core'=2] {'z_pair','x'}, dimensions={0} | all-to-all | bytes 3145728 | tf_op jit(solution)/shard_map/all_to_all | solution.py:19
  80.0 0.2 reduce_sum.36
  80.3 3.8 %collective-permute-start.1 = (bf16[64,1536]{1,0:T(8,128)(2,1)S(1)}, bf16[64,1536]{1,0:T(8,128)(2,1)S(1)}, u32[]{:S(2)}, u32[]{:S(2)}) collective-permute-start(bf16[64,1536]{1,0:T(8,128)(2,1)S(1)} %reduce_sum.36), channel_id=1, source_target_pairs={{0,256},{256,0},{1,257},{257,1},{2,258},{258,2},{3,259},{259,3},{4... | collective-permute-start | bytes 589832 | tf_op jit(solution)/shard_map/ppermute | solution.py:31
  84.1 6.9 %collective-permute-done.1 = bf16[64,1536]{1,0:T(8,128)(2,1)S(1)} collective-permute-done((bf16[64,1536]{1,0:T(8,128)(2,1)S(1)}, bf16[64,1536]{1,0:T(8,128)(2,1)S(1)}, u32[]{:S(2)}, u32[]{:S(2)}) %collective-permute-start.1) | collective-permute-done | bytes 196640 | tf_op jit(solution)/shard_map/ppermute | solution.py:31
  91.0 0.1 multiply_convert_fusion
  91.2 0.1 broadcast_in_dim.8
  91.3 26.4 %all_to_all.33 = bf16[8,64,1536]{2,1,0:T(8,128)(2,1)S(1)} all-to-all(bf16[8,64,1536]{2,1,0:T(8,128)(2,1)S(1)} %broadcast_in_dim.8), channel_id=1, replica_groups=mesh['z_half'=2,'z_pair'=2,'x'=4,'z_hi'=4,'y'=4,'core'=2] {'z_pair','x'}, dimensions={0} | all-to-all | bytes 3145728 | tf_op jit(solution)/shard_map/all_to_all | solution.py:19
  117.7 0.5 convolution_convert_fusion.4
  118.2 0.8 copy-done.4
  118.9 0.5 convolution_convert_fusion.5
  119.5 1.9 %collective-permute-start.2 = (bf16[256,1536]{1,0:T(8,128)(2,1)S(1)}, bf16[256,1536]{1,0:T(8,128)(2,1)S(1)}, u32[]{:S(2)}, u32[]{:S(2)}) collective-permute-start(bf16[256,1536]{1,0:T(8,128)(2,1)S(1)} %pad_maximum_fusion.2), channel_id=1, source_target_pairs={{0,1},{1,0},{2,3},{3,2},{4,5},{5,4},{6,7},{7,6},{8,9},{9,8},{10,11... | collective-permute-start | bytes 2359304 | tf_op jit(solution)/shard_map/ppermute | solution.py:31
  121.4 0.5 convolution_convert_fusion.6
  121.9 0.5 convolution_convert_fusion.7
  122.4 1.3 collective-permute-done.2
  123.7 0.2 add_convert_fusion
  123.9 15.3 %all_to_all.34 = bf16[4,64,1536]{2,1,0:T(8,128)(2,1)S(1)} all-to-all(bf16[4,64,1536]{2,1,0:T(8,128)(2,1)S(1)} %bitcast.12), channel_id=1, replica_groups=mesh['z_half'=2,'z_pair'=2,'x'=4,'z_hi'=4,'y'=4,'core'=2] {'y'}, dimensions={0} | all-to-all | bytes 1572864 | tf_op jit(solution)/shard_map/all_to_all | solution.py:19
  139.1 0.8 reduce_sum.37
  139.9 3.6 %all-to-all-start.5 = ((bf16[4,16,1536]{2,1,0:T(8,128)(2,1)}), bf16[4,16,1536]{2,1,0:T(8,128)(2,1)S(1)}, u32[]{:S(2)}, u32[]{:S(2)}) async-start(bf16[4,16,1536]{2,1,0:T(8,128)(2,1)} %bitcast.19), calls=%async_computation.5 | async-start | bytes 393216 | tf_op jit(solution)/shard_map/all_to_all | solution.py:19
  143.6 3.1 %convolution_convert_fusion = bf16[768,768]{1,0:T(8,128)(2,1)} fusion(bf16[512,1536]{1,0:T(8,128)(2,1)S(1)} %bitcast.17, bf16[256,1536]{1,0:T(8,128)(2,1)} %copy-done.5, bf16[256,1536]{1,0:T(8,128)(2,1)} %bitcast.23), kind=kOutput, calls=%fused_computation.4 | convolution fusion | flops 606142464 | bytes 3538944 | tf_op jit(solution)/shard_map/dot_general | solution.py:15
  146.6 1.8 %convolution_convert_fusion.1 = bf16[768,768]{1,0:T(8,128)(2,1)} fusion(bf16[512,1536]{1,0:T(8,128)(2,1)S(1)} %bitcast.18, bf16[256,1536]{1,0:T(8,128)(2,1)S(1)} %bitcast.24, bf16[256,1536]{1,0:T(8,128)(2,1)S(1)} %copy-done.6), kind=kOutput, calls=%fused_computation.5 | convolution fusion | flops 606142464 | bytes 3538944 | tf_op jit(solution)/shard_map/dot_general | solution.py:15
  148.5 12.3 %all-to-all-done.5 = bf16[4,16,1536]{2,1,0:T(8,128)(2,1)S(1)} async-done(((bf16[4,16,1536]{2,1,0:T(8,128)(2,1)}), bf16[4,16,1536]{2,1,0:T(8,128)(2,1)S(1)}, u32[]{:S(2)}, u32[]{:S(2)}) %all-to-all-start.5) | async-done | bytes 196640 | tf_op jit(solution)/shard_map/all_to_all | solution.py:19
  160.8 0.6 fusion.18
  (17 shorter events, 0.2 us)
Async XLA Ops:
  0.6 52.8 %copy-start = (bf16[768,768]{1,0:T(8,128)(2,1)S(1)}, bf16[768,768]{1,0:T(8,128)(2,1)}, u32[]{:S(2)}) copy-start(bf16[768,768]{1,0:T(8,128)(2,1)} %param.5) | copy-start | bytes 3538948
  1.5 51.1 %copy-start.3 = (bf16[768,768]{1,0:T(8,128)(2,1)S(1)}, bf16[768,768]{1,0:T(8,128)(2,1)}, u32[]{:S(2)}) copy-start(bf16[768,768]{1,0:T(8,128)(2,1)} %param.6) | copy-start | bytes 3538948
  48.4 5.0 %copy-start.1 = (bf16[4,4,16,1536]{3,2,1,0:T(8,128)(2,1)}, bf16[4,4,16,1536]{3,2,1,0:T(8,128)(2,1)S(1)}, u32[]{:S(2)}) copy-start(bf16[4,4,16,1536]{3,2,1,0:T(8,128)(2,1)S(1)} %all_to_all.31) | copy-start | bytes 2359300
  48.4 4.2 %collective-permute-start = (bf16[256,1536]{1,0:T(8,128)(2,1)S(1)}, bf16[256,1536]{1,0:T(8,128)(2,1)S(1)}, u32[]{:S(2)}, u32[]{:S(2)}) collective-permute-start(bf16[256,1536]{1,0:T(8,128)(2,1)S(1)} %bitcast.20), channel_id=1, source_target_pairs={{0,1},{1,0},{2,3},{3,2},{4,5},{5,4},{6,7},{7,6},{8,9},{9,8},{10,11... | collective-permute-start | bytes 2359304 | tf_op jit(solution)/shard_map/ppermute | solution.py:31
  52.6 0.9 copy-start.5
  80.3 10.7 %collective-permute-start.1 = (bf16[64,1536]{1,0:T(8,128)(2,1)S(1)}, bf16[64,1536]{1,0:T(8,128)(2,1)S(1)}, u32[]{:S(2)}, u32[]{:S(2)}) collective-permute-start(bf16[64,1536]{1,0:T(8,128)(2,1)S(1)} %reduce_sum.36), channel_id=1, source_target_pairs={{0,256},{256,0},{1,257},{257,1},{2,258},{258,2},{3,259},{259,3},{4... | collective-permute-start | bytes 589832 | tf_op jit(solution)/shard_map/ppermute | solution.py:31
  117.7 1.3 copy-start.4
  119.5 4.2 %collective-permute-start.2 = (bf16[256,1536]{1,0:T(8,128)(2,1)S(1)}, bf16[256,1536]{1,0:T(8,128)(2,1)S(1)}, u32[]{:S(2)}, u32[]{:S(2)}) collective-permute-start(bf16[256,1536]{1,0:T(8,128)(2,1)S(1)} %pad_maximum_fusion.2), channel_id=1, source_target_pairs={{0,1},{1,0},{2,3},{3,2},{4,5},{5,4},{6,7},{7,6},{8,9},{9,8},{10,11... | collective-permute-start | bytes 2359304 | tf_op jit(solution)/shard_map/ppermute | solution.py:31
  139.9 20.8 %all-to-all-start.5 = ((bf16[4,16,1536]{2,1,0:T(8,128)(2,1)}), bf16[4,16,1536]{2,1,0:T(8,128)(2,1)S(1)}, u32[]{:S(2)}, u32[]{:S(2)}) async-start(bf16[4,16,1536]{2,1,0:T(8,128)(2,1)} %bitcast.19), calls=%async_computation.5 | async-start | bytes 393216 | tf_op jit(solution)/shard_map/all_to_all | solution.py:19
  143.6 3.1 %copy-start.2 = (bf16[4,4,16,1536]{3,2,1,0:T(8,128)(2,1)S(1)}, bf16[4,4,16,1536]{3,2,1,0:T(8,128)(2,1)}, u32[]{:S(2)}) copy-start(bf16[4,4,16,1536]{3,2,1,0:T(8,128)(2,1)} %copy-done.1) | copy-start | bytes 2359300
  143.6 3.1 %copy-start.6 = (bf16[256,1536]{1,0:T(8,128)(2,1)S(1)}, bf16[256,1536]{1,0:T(8,128)(2,1)}, u32[]{:S(2)}) copy-start(bf16[256,1536]{1,0:T(8,128)(2,1)} %copy-done.5) | copy-start | bytes 2359300

commit v3 on v2

v3 whole, which is shorter than its diff:
```python
import jax
import jax.numpy as jnp
from jax import lax
from jax.sharding import Mesh, PartitionSpec as P

F32 = jnp.float32
BF16 = jnp.bfloat16


def gelu_tanh(values):
    return jax.nn.gelu(values, approximate=True)


def product(left, right, dims):
    return lax.dot_general(left, right, (dims, ((), ())), preferred_element_type=F32).astype(BF16)


def exchange(parts, axis):
    return lax.all_to_all(parts, axis, 0, 0)


def gather(share, axis, size):
    return exchange(jnp.broadcast_to(share[None], (size, *share.shape)), axis)


def summed(parts):
    return jnp.sum(parts.astype(F32), axis=0)


def swapped(values, axis):
    return lax.ppermute(values, axis, [(0, 1), (1, 0)])


def together(*values):
    return lax.optimization_barrier(values)


def per_device(inputs, w_in, w_out, cotangent):
    rows, width = inputs.shape
    units = w_in.shape[1]
    size = {name: lax.axis_size(name) for name in ("z_pair", "x", "z_hi", "y")}
    plane = size["z_pair"] * size["x"]

    def hidden_terms(tokens):
        terms = [
            product(tokens[:, :width], w_in, ((1,), (0,))),
            product(tokens[:, width:], w_out, ((1,), (1,))),
        ]
        return jnp.concatenate(terms, axis=1).reshape(plane, -1, 2 * units)

    def layer_terms(both):
        terms = [
            product(both[:, :units], w_out, ((1,), (0,))),
            product(both[:, units:], w_in, ((1,), (1,))),
        ]
        return jnp.concatenate(terms, axis=1)

    def row_part(terms):
        return summed(exchange(terms, ("z_pair", "x"))).astype(BF16)

    def copies(part):
        both = part.astype(F32) + swapped(part, "z_half").astype(F32)
        active, pullback = jax.vjp(gelu_tanh, both[:, :units])
        share = jnp.concatenate([active.astype(BF16), pullback(both[:, units:])[0].astype(BF16)], axis=1)
        return jnp.broadcast_to(share[None], (plane, *share.shape))

    share = jnp.concatenate([inputs, cotangent], axis=1)
    own = gather(gather(share, "z_hi", size["z_hi"]), "y", size["y"]).reshape(-1, 2 * width)
    other = swapped(own, "core")
    own_terms, terms = together(hidden_terms(own), hidden_terms(other))
    other_part = row_part(terms)
    own_part = row_part(own_terms)
    share, own_part = together(copies(other_part), own_part)
    other_both = exchange(share, ("z_pair", "x"))
    share, other_both = together(copies(own_part), other_both)
    own_both = exchange(share, ("z_pair", "x")).reshape(-1, 2 * units)
    other_both = other_both.reshape(-1, 2 * units)

    kept = layer_terms(own_both)
    arriving = swapped(layer_terms(other_both), "core")
    parts = (kept.astype(F32) + arriving.astype(F32)).astype(BF16)
    parts = exchange(parts.reshape(size["y"], -1, 2 * width), "y")
    parts = summed(parts).astype(BF16).reshape(size["z_hi"], -1, 2 * width)
    output = summed(exchange(parts, "z_hi")).astype(BF16)

    tokens = jnp.concatenate([own, other], axis=0)
    both = jnp.concatenate([own_both, other_both], axis=0)
    grad_w_in = product(tokens[:, :width], both[:, units:], ((0,), (0,)))
    grad_w_out = product(both[:, :units], tokens[:, width:], ((0,), (0,)))
    return output[:, :width], output[:, width:], grad_w_in, grad_w_out


def solution(mesh):
    names = ("z_half", "z_pair", "x", "z_hi", "y", "core")
    fine = Mesh(mesh.devices.reshape(2, 2, 4, 4, 4, 2), names)
    row, col = names[:3], names[3:]
    return jax.shard_map(
        per_device,
        mesh=fine,
        in_specs=(P(col, row), P(row, col), P(col, row), P(col, row)),
        out_specs=(P(col, row), P(col, row), P(row, col), P(col, row)),
        check_vma=False,
    )
```

time: 162 us -> 158 us (0.975)
  the two profiles are of different devices: /device:TPU:64 before, /device:TPU:34 now
where the time goes in v3:
time: 158 us; the launch traced here: 157 us
  blocking collectives  76.8 us (49%)
  starting transfers between devices  29.6 us (19%)
  waiting for transfers between devices  29.5 us (19%)
  matrix products  8.81 us (6%)
  other arithmetic  6.92 us (4%)
  local copies, waits for them, and re-layouts  4.43 us (3%)
    all_to_all x4, blocking collectives, exchange(): return lax.all_to_all(parts, axis, 0, 0)  76.8 us
    all_to_all x4, starting transfers between devices, exchange(): return lax.all_to_all(parts, axis, 0, 0)  20.4 us
    all_to_all x4, waiting for transfers between devices, exchange(): return lax.all_to_all(parts, axis, 0, 0)  20.3 us
    ppermute x4, starting transfers between devices, swapped(): return lax.ppermute(values, axis, [(0, 1), (1, 0)])  9.28 us
    ppermute x4, waiting for transfers between devices, swapped(): return lax.ppermute(values, axis, [(0, 1), (1, 0)])  9.22 us
    dot_general x10, matrix products, product(): lax.dot_general(left, right, (dims, ((), ())), preferred_element_type=F32)  8.81 us
  transfers between devices with their start and end apart: 8, of which 6 were waited for; matrix products, arithmetic and copies ran while one was open for 7% of the time, Pallas kernels for 0%

profile of v3, /device:TPU:34, one launch (start us, length us, event | category | flops | bytes accessed | tf_op | source)
XLA Modules:
  0.0 157.0 jit_solution(4235658381797951487)
XLA Ops:
  0.6 0.9 pad_maximum_fusion.9
  1.5 32.8 %all_to_all.40 = bf16[4,16,1536]{2,1,0:T(8,128)(2,1)S(1)} all-to-all(bf16[4,16,1536]{2,1,0:T(8,128)(2,1)S(1)} %broadcast_in_dim.8), channel_id=1, replica_groups=mesh['z_half'=2,'z_pair'=2,'x'=4,'z_hi'=4,'y'=4,'core'=2] {'z_hi'}, dimensions={0} | all-to-all | bytes 393216 | tf_op jit(solution)/shard_map/all_to_all | solution.py:19
  34.4 14.9 %all_to_all.41 = bf16[4,4,16,1536]{3,2,1,0:T(8,128)(2,1)S(1)} all-to-all(bf16[4,4,16,1536]{3,2,1,0:T(8,128)(2,1)S(1)} %broadcast_in_dim.9), channel_id=1, replica_groups=mesh['z_half'=2,'z_pair'=2,'x'=4,'z_hi'=4,'y'=4,'core'=2] {'y'}, dimensions={0} | all-to-all | bytes 1572864 | tf_op jit(solution)/shard_map/all_to_all | solution.py:19
  49.3 1.9 %collective-permute-start = (bf16[256,1536]{1,0:T(8,128)(2,1)S(1)}, bf16[256,1536]{1,0:T(8,128)(2,1)S(1)}, u32[]{:S(2)}, u32[]{:S(2)}) collective-permute-start(bf16[256,1536]{1,0:T(8,128)(2,1)S(1)} %bitcast.17), channel_id=1, source_target_pairs={{0,1},{1,0},{2,3},{3,2},{4,5},{5,4},{6,7},{7,6},{8,9},{9,8},{10,11... | collective-permute-start | bytes 2359304 | tf_op jit(solution)/shard_map/ppermute | solution.py:31
  51.2 0.5 convolution_convert_fusion.8
  52.2 0.9 pad_maximum_fusion.4
  54.5 16.7 %all_to_all.42 = bf16[8,32,1536]{2,1,0:T(8,128)(2,1)S(1)} all-to-all(bf16[8,32,1536]{2,1,0:T(8,128)(2,1)S(1)} %bitcast.15), channel_id=1, replica_groups=mesh['z_half'=2,'z_pair'=2,'x'=4,'z_hi'=4,'y'=4,'core'=2] {'z_pair','x'}, dimensions={0} | all-to-all | bytes 1572864 | tf_op jit(solution)/shard_map/all_to_all | solution.py:19
  71.3 5.5 %all-to-all-start.3 = ((bf16[8,32,1536]{2,1,0:T(8,128)(2,1)}), bf16[8,32,1536]{2,1,0:T(8,128)(2,1)S(1)}, u32[]{:S(2)}, u32[]{:S(2)}) async-start(bf16[8,32,1536]{2,1,0:T(8,128)(2,1)} %bitcast.1), calls=%async_computation.3 | async-start | bytes 1572864 | tf_op jit(solution)/shard_map/all_to_all | solution.py:19
  76.7 0.8 reduce_sum.48
  77.5 2.9 %collective-permute-start.1 = (bf16[32,1536]{1,0:T(8,128)(2,1)}, bf16[32,1536]{1,0:T(8,128)(2,1)S(1)}, u32[]{:S(2)}, u32[]{:S(2)}) collective-permute-start(bf16[32,1536]{1,0:T(8,128)(2,1)} %reduce_sum.48), channel_id=1, source_target_pairs={{0,256},{256,0},{1,257},{257,1},{2,258},{258,2},{3,259},{259,3},{4... | collective-permute-start | bytes 294920 | tf_op jit(solution)/shard_map/ppermute | solution.py:31
  80.4 6.1 %all-to-all-done.3 = bf16[8,32,1536]{2,1,0:T(8,128)(2,1)S(1)} async-done(((bf16[8,32,1536]{2,1,0:T(8,128)(2,1)}), bf16[8,32,1536]{2,1,0:T(8,128)(2,1)S(1)}, u32[]{:S(2)}, u32[]{:S(2)}) %all-to-all-start.3) | async-done | bytes 786464 | tf_op jit(solution)/shard_map/all_to_all | solution.py:19
  86.6 1.3 collective-permute-done.1
  87.9 0.9 convert_add_fusion.1
  88.9 0.9 broadcast_in_dim.10
  89.9 5.8 %all-to-all-start.4 = ((bf16[8,32,1536]{2,1,0:T(8,128)(2,1)}), bf16[8,32,1536]{2,1,0:T(8,128)(2,1)S(1)}, u32[]{:S(2)}, u32[]{:S(2)}) async-start(bf16[8,32,1536]{2,1,0:T(8,128)(2,1)} %broadcast_in_dim.10), calls=%async_computation.4 | async-start | bytes 1572864 | tf_op jit(solution)/shard_map/all_to_all | solution.py:19
  95.6 2.5 %collective-permute-start.2 = (bf16[32,1536]{1,0:T(8,128)(2,1)S(1)}, bf16[32,1536]{1,0:T(8,128)(2,1)S(1)}, u32[]{:S(2)}, u32[]{:S(2)}) collective-permute-start(bf16[32,1536]{1,0:T(8,128)(2,1)S(1)} %reduce_sum.49), channel_id=1, source_target_pairs={{0,256},{256,0},{1,257},{257,1},{2,258},{258,2},{3,259},{259,3},{4... | collective-permute-start | bytes 294920 | tf_op jit(solution)/shard_map/ppermute | solution.py:31
  98.2 7.6 %collective-permute-done.2 = bf16[32,1536]{1,0:T(8,128)(2,1)S(1)} collective-permute-done((bf16[32,1536]{1,0:T(8,128)(2,1)S(1)}, bf16[32,1536]{1,0:T(8,128)(2,1)S(1)}, u32[]{:S(2)}, u32[]{:S(2)}) %collective-permute-start.2) | collective-permute-done | bytes 98336 | tf_op jit(solution)/shard_map/ppermute | solution.py:31
  106.0 0.9 broadcast_in_dim.11
  106.9 5.8 %all-to-all-start.5 = ((bf16[8,32,1536]{2,1,0:T(8,128)(2,1)}), bf16[8,32,1536]{2,1,0:T(8,128)(2,1)S(1)}, u32[]{:S(2)}, u32[]{:S(2)}) async-start(bf16[8,32,1536]{2,1,0:T(8,128)(2,1)} %broadcast_in_dim.11), calls=%async_computation.5 | async-start | bytes 1572864 | tf_op jit(solution)/shard_map/all_to_all | solution.py:19
  113.2 0.8 copy-done.4
  114.4 0.9 pad_maximum_fusion.6
  115.3 1.9 %collective-permute-start.3 = (bf16[256,1536]{1,0:T(8,128)(2,1)}, bf16[256,1536]{1,0:T(8,128)(2,1)}, u32[]{:S(2)}, u32[]{:S(2)}) collective-permute-start(bf16[256,1536]{1,0:T(8,128)(2,1)} %pad_maximum_fusion.6), channel_id=1, source_target_pairs={{0,1},{1,0},{2,3},{3,2},{4,5},{5,4},{6,7},{7,6},{8,9},{9,8},{10,11... | collective-permute-start | bytes 2359304 | tf_op jit(solution)/shard_map/ppermute | solution.py:31
  117.3 3.5 %all-to-all-done.5 = bf16[8,32,1536]{2,1,0:T(8,128)(2,1)S(1)} async-done(((bf16[8,32,1536]{2,1,0:T(8,128)(2,1)}), bf16[8,32,1536]{2,1,0:T(8,128)(2,1)S(1)}, u32[]{:S(2)}, u32[]{:S(2)}) %all-to-all-start.5) | async-done | bytes 786464 | tf_op jit(solution)/shard_map/all_to_all | solution.py:19
  121.2 1.0 copy-done.5
  122.8 1.3 add_convert_fusion
  124.1 12.3 %all_to_all.43 = bf16[4,64,1536]{2,1,0:T(8,128)(2,1)S(1)} all-to-all(bf16[4,64,1536]{2,1,0:T(8,128)(2,1)S(1)} %bitcast.16), channel_id=1, replica_groups=mesh['z_half'=2,'z_pair'=2,'x'=4,'z_hi'=4,'y'=4,'core'=2] {'y'}, dimensions={0} | all-to-all | bytes 1572864 | tf_op jit(solution)/shard_map/all_to_all | solution.py:19
  136.5 0.8 reduce_sum.50
  137.3 3.4 %all-to-all-start.7 = ((bf16[4,16,1536]{2,1,0:T(8,128)(2,1)}), bf16[4,16,1536]{2,1,0:T(8,128)(2,1)S(1)}, u32[]{:S(2)}, u32[]{:S(2)}) async-start(bf16[4,16,1536]{2,1,0:T(8,128)(2,1)} %bitcast.6), calls=%async_computation.7 | async-start | bytes 393216 | tf_op jit(solution)/shard_map/all_to_all | solution.py:19
  140.7 3.1 %convolution_convert_fusion = bf16[768,768]{1,0:T(8,128)(2,1)} fusion(bf16[256,1536]{1,0:T(8,128)(2,1)} %copy-done.6, bf16[256,1536]{1,0:T(8,128)(2,1)S(1)} %bitcast.20, bf16[256,1536]{1,0:T(8,128)(2,1)S(1)} %bitcast.24, bf16[256,1536]{1,0:T(8,128)(2,1)} %bitcast.28), kind=kOutput, calls=%fused_computation.5 | convolution fusion | flops 607715328 | bytes 4325376 | tf_op jit(solution)/shard_map/dot_general | solution.py:15
  143.7 1.8 %convolution_convert_fusion.1 = bf16[768,768]{1,0:T(8,128)(2,1)} fusion(bf16[256,1536]{1,0:T(8,128)(2,1)S(1)} %bitcast.29, bf16[256,1536]{1,0:T(8,128)(2,1)S(1)} %bitcast.25, bf16[256,1536]{1,0:T(8,128)(2,1)S(1)} %bitcast.21, bf16[256,1536]{1,0:T(8,128)(2,1)S(1)} %copy-done.7), kind=kOutput, calls=%fused_computation.6 | convolution fusion | flops 607715328 | bytes 4325376 | tf_op jit(solution)/shard_map/dot_general | solution.py:15
  145.6 10.8 %all-to-all-done.7 = bf16[4,16,1536]{2,1,0:T(8,128)(2,1)S(1)} async-done(((bf16[4,16,1536]{2,1,0:T(8,128)(2,1)}), bf16[4,16,1536]{2,1,0:T(8,128)(2,1)S(1)}, u32[]{:S(2)}, u32[]{:S(2)}) %all-to-all-start.7) | async-done | bytes 196640 | tf_op jit(solution)/shard_map/all_to_all | solution.py:19
  156.4 0.6 fusion.30
  (34 shorter events, 4.2 us)
Async XLA Ops:
  0.6 51.1 %copy-start = (bf16[768,768]{1,0:T(8,128)(2,1)S(1)}, bf16[768,768]{1,0:T(8,128)(2,1)}, u32[]{:S(2)}) copy-start(bf16[768,768]{1,0:T(8,128)(2,1)} %param.5) | copy-start | bytes 3538948
  34.3 16.9 %copy-start.3 = (bf16[768,768]{1,0:T(8,128)(2,1)S(1)}, bf16[768,768]{1,0:T(8,128)(2,1)}, u32[]{:S(2)}) copy-start(bf16[768,768]{1,0:T(8,128)(2,1)} %param.6) | copy-start | bytes 3538948
  49.3 4.2 %collective-permute-start = (bf16[256,1536]{1,0:T(8,128)(2,1)S(1)}, bf16[256,1536]{1,0:T(8,128)(2,1)S(1)}, u32[]{:S(2)}, u32[]{:S(2)}) collective-permute-start(bf16[256,1536]{1,0:T(8,128)(2,1)S(1)} %bitcast.17), channel_id=1, source_target_pairs={{0,1},{1,0},{2,3},{3,2},{4,5},{5,4},{6,7},{7,6},{8,9},{9,8},{10,11... | collective-permute-start | bytes 2359304 | tf_op jit(solution)/shard_map/ppermute | solution.py:31
  53.5 1.0 copy-start.6
  71.3 15.3 %all-to-all-start.3 = ((bf16[8,32,1536]{2,1,0:T(8,128)(2,1)}), bf16[8,32,1536]{2,1,0:T(8,128)(2,1)S(1)}, u32[]{:S(2)}, u32[]{:S(2)}) async-start(bf16[8,32,1536]{2,1,0:T(8,128)(2,1)} %bitcast.1), calls=%async_computation.3 | async-start | bytes 1572864 | tf_op jit(solution)/shard_map/all_to_all | solution.py:19
  77.5 10.4 %collective-permute-start.1 = (bf16[32,1536]{1,0:T(8,128)(2,1)}, bf16[32,1536]{1,0:T(8,128)(2,1)S(1)}, u32[]{:S(2)}, u32[]{:S(2)}) collective-permute-start(bf16[32,1536]{1,0:T(8,128)(2,1)} %reduce_sum.48), channel_id=1, source_target_pairs={{0,256},{256,0},{1,257},{257,1},{2,258},{258,2},{3,259},{259,3},{4... | collective-permute-start | bytes 294920 | tf_op jit(solution)/shard_map/ppermute | solution.py:31
  89.9 16.1 %all-to-all-start.4 = ((bf16[8,32,1536]{2,1,0:T(8,128)(2,1)}), bf16[8,32,1536]{2,1,0:T(8,128)(2,1)S(1)}, u32[]{:S(2)}, u32[]{:S(2)}) async-start(bf16[8,32,1536]{2,1,0:T(8,128)(2,1)} %broadcast_in_dim.10), calls=%async_computation.4 | async-start | bytes 1572864 | tf_op jit(solution)/shard_map/all_to_all | solution.py:19
  95.6 10.2 %collective-permute-start.2 = (bf16[32,1536]{1,0:T(8,128)(2,1)S(1)}, bf16[32,1536]{1,0:T(8,128)(2,1)S(1)}, u32[]{:S(2)}, u32[]{:S(2)}) collective-permute-start(bf16[32,1536]{1,0:T(8,128)(2,1)S(1)} %reduce_sum.49), channel_id=1, source_target_pairs={{0,256},{256,0},{1,257},{257,1},{2,258},{258,2},{3,259},{259,3},{4... | collective-permute-start | bytes 294920 | tf_op jit(solution)/shard_map/ppermute | solution.py:31
  106.9 13.8 %all-to-all-start.5 = ((bf16[8,32,1536]{2,1,0:T(8,128)(2,1)}), bf16[8,32,1536]{2,1,0:T(8,128)(2,1)S(1)}, u32[]{:S(2)}, u32[]{:S(2)}) async-start(bf16[8,32,1536]{2,1,0:T(8,128)(2,1)} %broadcast_in_dim.11), calls=%async_computation.5 | async-start | bytes 1572864 | tf_op jit(solution)/shard_map/all_to_all | solution.py:19
  112.6 1.3 copy-start.4
  115.3 7.4 %collective-permute-start.3 = (bf16[256,1536]{1,0:T(8,128)(2,1)}, bf16[256,1536]{1,0:T(8,128)(2,1)}, u32[]{:S(2)}, u32[]{:S(2)}) collective-permute-start(bf16[256,1536]{1,0:T(8,128)(2,1)} %pad_maximum_fusion.6), channel_id=1, source_target_pairs={{0,1},{1,0},{2,3},{3,2},{4,5},{5,4},{6,7},{7,6},{8,9},{9,8},{10,11... | collective-permute-start | bytes 2359304 | tf_op jit(solution)/shard_map/ppermute | solution.py:31
  120.7 2.0 %copy-start.1 = (bf16[8,32,1536]{2,1,0:T(8,128)(2,1)}, bf16[8,32,1536]{2,1,0:T(8,128)(2,1)S(1)}, u32[]{:S(2)}) copy-start(bf16[8,32,1536]{2,1,0:T(8,128)(2,1)S(1)} %all-to-all-done.5) | copy-start | bytes 2359300
  120.7 1.6 copy-start.5
  137.3 19.1 %all-to-all-start.7 = ((bf16[4,16,1536]{2,1,0:T(8,128)(2,1)}), bf16[4,16,1536]{2,1,0:T(8,128)(2,1)S(1)}, u32[]{:S(2)}, u32[]{:S(2)}) async-start(bf16[4,16,1536]{2,1,0:T(8,128)(2,1)} %bitcast.6), calls=%async_computation.7 | async-start | bytes 393216 | tf_op jit(solution)/shard_map/all_to_all | solution.py:19
  140.7 3.1 %copy-start.2 = (bf16[8,32,1536]{2,1,0:T(8,128)(2,1)S(1)}, bf16[8,32,1536]{2,1,0:T(8,128)(2,1)}, u32[]{:S(2)}) copy-start(bf16[8,32,1536]{2,1,0:T(8,128)(2,1)} %copy-done.1) | copy-start | bytes 2359300
  140.7 3.1 %copy-start.7 = (bf16[256,1536]{1,0:T(8,128)(2,1)S(1)}, bf16[256,1536]{1,0:T(8,128)(2,1)}, u32[]{:S(2)}) copy-start(bf16[256,1536]{1,0:T(8,128)(2,1)} %copy-done.6) | copy-start | bytes 2359300

commit v4 on v3

--- a/solution.py
+++ b/solution.py
@@ -49,11 +49,10 @@
         return jnp.concatenate(terms, axis=1).reshape(plane, -1, 2 * units)
 
     def layer_terms(both):
-        terms = [
-            product(both[:, :units], w_out, ((1,), (0,))),
-            product(both[:, units:], w_in, ((1,), (1,))),
-        ]
-        return jnp.concatenate(terms, axis=1)
+        return (
+            lax.dot_general(both[:, :units], w_out, (((1,), (0,)), ((), ())), preferred_element_type=F32),
+            lax.dot_general(both[:, units:], w_in, (((1,), (1,)), ((), ())), preferred_element_type=F32),
+        )
 
     def row_part(terms):
         return summed(exchange(terms, ("z_pair", "x"))).astype(BF16)
@@ -76,9 +75,10 @@
     own_both = exchange(share, ("z_pair", "x")).reshape(-1, 2 * units)
     other_both = other_both.reshape(-1, 2 * units)
 
-    kept = layer_terms(own_both)
-    arriving = swapped(layer_terms(other_both), "core")
-    parts = (kept.astype(F32) + arriving.astype(F32)).astype(BF16)
+    arriving = swapped(jnp.concatenate([term.astype(BF16) for term in layer_terms(other_both)], axis=1), "core")
+    arriving = [arriving[:, :width], arriving[:, width:]]
+    parts = [(kept + term.astype(F32)).astype(BF16) for kept, term in zip(layer_terms(own_both), arriving)]
+    parts = jnp.concatenate(parts, axis=1)
     parts = exchange(parts.reshape(size["y"], -1, 2 * width), "y")
     parts = summed(parts).astype(BF16).reshape(size["z_hi"], -1, 2 * width)
     output = summed(exchange(parts, "z_hi")).astype(BF16)

time: 158 us -> 160 us (1.013)
  the two profiles are of different devices: /device:TPU:34 before, /device:TPU:38 now
where the time goes in v4:
time: 160 us; the launch traced here: 159 us
  blocking collectives  78.1 us (49%)
  starting transfers between devices  30.4 us (19%)
  waiting for transfers between devices  29.9 us (19%)
  matrix products  12.4 us (8%)
  other arithmetic  4.77 us (3%)
  local copies, waits for them, and re-layouts  2.62 us (2%)
    all_to_all x4, blocking collectives, exchange(): return lax.all_to_all(parts, axis, 0, 0)  78.1 us
    all_to_all x4, starting transfers between devices, exchange(): return lax.all_to_all(parts, axis, 0, 0)  21 us
    all_to_all x4, waiting for transfers between devices, exchange(): return lax.all_to_all(parts, axis, 0, 0)  18 us
    ppermute x4, waiting for transfers between devices, swapped(): return lax.ppermute(values, axis, [(0, 1), (1, 0)])  11.8 us
    ppermute x4, starting transfers between devices, swapped(): return lax.ppermute(values, axis, [(0, 1), (1, 0)])  9.42 us
    dot_general x6, matrix products, product(): lax.dot_general(left, right, (dims, ((), ())), preferred_element_type=F32)  6.85 us
    dot_general x2, matrix products, layer_terms(): lax.dot_general(both[:, units:], w_in, (((1,), (1,)), ((), ())), preferre...  3.27 us
  transfers between devices with their start and end apart: 8, of which 7 were waited for; matrix products, arithmetic and copies ran while one was open for 6% of the time, Pallas kernels for 0%

profile of v4, /device:TPU:38, one launch (start us, length us, event | category | flops | bytes accessed | tf_op | source)
XLA Modules:
  0.0 159.0 jit_solution(2854205301657741391)
XLA Ops:
  0.6 0.9 pad_maximum_fusion.10
  1.5 32.8 %all_to_all.40 = bf16[4,16,1536]{2,1,0:T(8,128)(2,1)S(1)} all-to-all(bf16[4,16,1536]{2,1,0:T(8,128)(2,1)S(1)} %broadcast_in_dim.8), channel_id=1, replica_groups=mesh['z_half'=2,'z_pair'=2,'x'=4,'z_hi'=4,'y'=4,'core'=2] {'z_hi'}, dimensions={0} | all-to-all | bytes 393216 | tf_op jit(solution)/shard_map/all_to_all | solution.py:19
  34.4 14.8 %all_to_all.41 = bf16[4,4,16,1536]{3,2,1,0:T(8,128)(2,1)S(1)} all-to-all(bf16[4,4,16,1536]{3,2,1,0:T(8,128)(2,1)S(1)} %broadcast_in_dim.9), channel_id=1, replica_groups=mesh['z_half'=2,'z_pair'=2,'x'=4,'z_hi'=4,'y'=4,'core'=2] {'y'}, dimensions={0} | all-to-all | bytes 1572864 | tf_op jit(solution)/shard_map/all_to_all | solution.py:19
  49.2 2.0 %collective-permute-start = (bf16[256,1536]{1,0:T(8,128)(2,1)S(1)}, bf16[256,1536]{1,0:T(8,128)(2,1)S(1)}, u32[]{:S(2)}, u32[]{:S(2)}) collective-permute-start(bf16[256,1536]{1,0:T(8,128)(2,1)S(1)} %bitcast.17), channel_id=1, source_target_pairs={{0,1},{1,0},{2,3},{3,2},{4,5},{5,4},{6,7},{7,6},{8,9},{9,8},{10,11... | collective-permute-start | bytes 2359304 | tf_op jit(solution)/shard_map/ppermute | solution.py:31
  52.2 0.9 pad_maximum_fusion.4
  53.5 0.5 convolution_convert_fusion.4
  54.5 16.0 %all_to_all.42 = bf16[8,32,1536]{2,1,0:T(8,128)(2,1)S(1)} all-to-all(bf16[8,32,1536]{2,1,0:T(8,128)(2,1)S(1)} %bitcast.15), channel_id=1, replica_groups=mesh['z_half'=2,'z_pair'=2,'x'=4,'z_hi'=4,'y'=4,'core'=2] {'z_pair','x'}, dimensions={0} | all-to-all | bytes 1572864 | tf_op jit(solution)/shard_map/all_to_all | solution.py:19
  70.6 6.1 %all-to-all-start.3 = ((bf16[8,32,1536]{2,1,0:T(8,128)(2,1)}), bf16[8,32,1536]{2,1,0:T(8,128)(2,1)S(1)}, u32[]{:S(2)}, u32[]{:S(2)}) async-start(bf16[8,32,1536]{2,1,0:T(8,128)(2,1)} %bitcast.1), calls=%async_computation.3 | async-start | bytes 1572864 | tf_op jit(solution)/shard_map/all_to_all | solution.py:19
  76.7 0.8 reduce_sum.48
  77.5 2.9 %collective-permute-start.1 = (bf16[32,1536]{1,0:T(8,128)(2,1)}, bf16[32,1536]{1,0:T(8,128)(2,1)S(1)}, u32[]{:S(2)}, u32[]{:S(2)}) collective-permute-start(bf16[32,1536]{1,0:T(8,128)(2,1)} %reduce_sum.48), channel_id=1, source_target_pairs={{0,256},{256,0},{1,257},{257,1},{2,258},{258,2},{3,259},{259,3},{4... | collective-permute-start | bytes 294920 | tf_op jit(solution)/shard_map/ppermute | solution.py:31
  80.4 5.9 %all-to-all-done.3 = bf16[8,32,1536]{2,1,0:T(8,128)(2,1)S(1)} async-done(((bf16[8,32,1536]{2,1,0:T(8,128)(2,1)}), bf16[8,32,1536]{2,1,0:T(8,128)(2,1)S(1)}, u32[]{:S(2)}, u32[]{:S(2)}) %all-to-all-start.3) | async-done | bytes 786464 | tf_op jit(solution)/shard_map/all_to_all | solution.py:19
  86.3 1.5 collective-permute-done.1
  87.9 0.9 convert_add_fusion.1
  88.9 0.9 broadcast_in_dim.10
  89.8 5.8 %all-to-all-start.4 = ((bf16[8,32,1536]{2,1,0:T(8,128)(2,1)}), bf16[8,32,1536]{2,1,0:T(8,128)(2,1)S(1)}, u32[]{:S(2)}, u32[]{:S(2)}) async-start(bf16[8,32,1536]{2,1,0:T(8,128)(2,1)} %broadcast_in_dim.10), calls=%async_computation.4 | async-start | bytes 1572864 | tf_op jit(solution)/shard_map/all_to_all | solution.py:19
  95.6 2.5 %collective-permute-start.2 = (bf16[32,1536]{1,0:T(8,128)(2,1)S(1)}, bf16[32,1536]{1,0:T(8,128)(2,1)S(1)}, u32[]{:S(2)}, u32[]{:S(2)}) collective-permute-start(bf16[32,1536]{1,0:T(8,128)(2,1)S(1)} %reduce_sum.49), channel_id=1, source_target_pairs={{0,256},{256,0},{1,257},{257,1},{2,258},{258,2},{3,259},{259,3},{4... | collective-permute-start | bytes 294920 | tf_op jit(solution)/shard_map/ppermute | solution.py:31
  98.1 7.6 %collective-permute-done.2 = bf16[32,1536]{1,0:T(8,128)(2,1)S(1)} collective-permute-done((bf16[32,1536]{1,0:T(8,128)(2,1)S(1)}, bf16[32,1536]{1,0:T(8,128)(2,1)S(1)}, u32[]{:S(2)}, u32[]{:S(2)}) %collective-permute-start.2) | collective-permute-done | bytes 98336 | tf_op jit(solution)/shard_map/ppermute | solution.py:31
  105.9 0.9 broadcast_in_dim.11
  106.8 5.8 %all-to-all-start.5 = ((bf16[8,32,1536]{2,1,0:T(8,128)(2,1)}), bf16[8,32,1536]{2,1,0:T(8,128)(2,1)S(1)}, u32[]{:S(2)}, u32[]{:S(2)}) async-start(bf16[8,32,1536]{2,1,0:T(8,128)(2,1)} %broadcast_in_dim.11), calls=%async_computation.5 | async-start | bytes 1572864 | tf_op jit(solution)/shard_map/all_to_all | solution.py:19
  112.6 1.8 %convolution_convert_fusion.2 = bf16[256,768]{1,0:T(8,128)(2,1)S(1)} fusion(bf16[768,768]{1,0:T(8,128)(2,1)} %param.5, bf16[256,1536]{1,0:T(8,128)(2,1)S(1)} %bitcast.22), kind=kOutput, calls=%fused_computation.6 | convolution fusion | flops 302186496 | bytes 1966080 | tf_op jit(solution)/shard_map/dot_general | solution.py:54
  114.9 1.9 %collective-permute-start.3 = (bf16[256,1536]{1,0:T(8,128)(2,1)S(1)}, bf16[256,1536]{1,0:T(8,128)(2,1)}, u32[]{:S(2)}, u32[]{:S(2)}) collective-permute-start(bf16[256,1536]{1,0:T(8,128)(2,1)S(1)} %pad_maximum_fusion.6), channel_id=1, source_target_pairs={{0,1},{1,0},{2,3},{3,2},{4,5},{5,4},{6,7},{7,6},{8,9},{9,8},{10,11... | collective-permute-start | bytes 2359304 | tf_op jit(solution)/shard_map/ppermute | solution.py:31
  116.8 2.4 %collective-permute-done.3 = bf16[256,1536]{1,0:T(8,128)(2,1)} collective-permute-done((bf16[256,1536]{1,0:T(8,128)(2,1)S(1)}, bf16[256,1536]{1,0:T(8,128)(2,1)}, u32[]{:S(2)}, u32[]{:S(2)}) %collective-permute-start.3) | collective-permute-done | bytes 786464 | tf_op jit(solution)/shard_map/ppermute | solution.py:31
  119.2 0.8 all-to-all-done.5
  120.1 1.8 %add_convert_fusion.1 = bf16[256,768]{1,0:T(8,128)(2,1)S(1)} fusion(bf16[256,1536]{1,0:T(8,128)(2,1)} %collective-permute-done.3, bf16[768,768]{1,0:T(8,128)(2,1)S(1)} %copy-done, bf16[256,1536]{1,0:T(8,128)(2,1)S(1)} %bitcast.26), kind=kOutput, calls=%fused_computation.23 | convolution fusion | flops 302579712 | bytes 2359296 | tf_op jit(solution)/shard_map/dot_general | solution.py:53
  121.9 1.5 add_convert_fusion
  123.5 14.4 %all_to_all.43 = bf16[4,64,1536]{2,1,0:T(8,128)(2,1)S(1)} all-to-all(bf16[4,64,1536]{2,1,0:T(8,128)(2,1)S(1)} %bitcast.16), channel_id=1, replica_groups=mesh['z_half'=2,'z_pair'=2,'x'=4,'z_hi'=4,'y'=4,'core'=2] {'y'}, dimensions={0} | all-to-all | bytes 1572864 | tf_op jit(solution)/shard_map/all_to_all | solution.py:19
  137.9 0.8 reduce_sum.50
  138.7 3.4 %all-to-all-start.7 = ((bf16[4,16,1536]{2,1,0:T(8,128)(2,1)}), bf16[4,16,1536]{2,1,0:T(8,128)(2,1)S(1)}, u32[]{:S(2)}, u32[]{:S(2)}) async-start(bf16[4,16,1536]{2,1,0:T(8,128)(2,1)} %bitcast.6), calls=%async_computation.7 | async-start | bytes 393216 | tf_op jit(solution)/shard_map/all_to_all | solution.py:19
  142.1 3.1 %convolution_convert_fusion = bf16[768,768]{1,0:T(8,128)(2,1)} fusion(bf16[256,1536]{1,0:T(8,128)(2,1)} %copy-done.5, bf16[256,1536]{1,0:T(8,128)(2,1)S(1)} %bitcast.20, bf16[256,1536]{1,0:T(8,128)(2,1)S(1)} %bitcast.24, bf16[256,1536]{1,0:T(8,128)(2,1)} %bitcast.28), kind=kOutput, calls=%fused_computation.4 | convolution fusion | flops 607715328 | bytes 4325376 | tf_op jit(solution)/shard_map/dot_general | solution.py:15
  145.2 1.8 %convolution_convert_fusion.1 = bf16[768,768]{1,0:T(8,128)(2,1)} fusion(bf16[256,1536]{1,0:T(8,128)(2,1)S(1)} %bitcast.29, bf16[256,1536]{1,0:T(8,128)(2,1)S(1)} %bitcast.25, bf16[256,1536]{1,0:T(8,128)(2,1)S(1)} %bitcast.21, bf16[256,1536]{1,0:T(8,128)(2,1)S(1)} %copy-done.6), kind=kOutput, calls=%fused_computation.5 | convolution fusion | flops 607715328 | bytes 4325376 | tf_op jit(solution)/shard_map/dot_general | solution.py:15
  147.0 11.3 %all-to-all-done.7 = bf16[4,16,1536]{2,1,0:T(8,128)(2,1)S(1)} async-done(((bf16[4,16,1536]{2,1,0:T(8,128)(2,1)}), bf16[4,16,1536]{2,1,0:T(8,128)(2,1)S(1)}, u32[]{:S(2)}, u32[]{:S(2)}) %all-to-all-start.7) | async-done | bytes 196640 | tf_op jit(solution)/shard_map/all_to_all | solution.py:19
  158.4 0.6 fusion.36
  (32 shorter events, 2.9 us)
Async XLA Ops:
  0.6 50.6 %copy-start = (bf16[768,768]{1,0:T(8,128)(2,1)S(1)}, bf16[768,768]{1,0:T(8,128)(2,1)}, u32[]{:S(2)}) copy-start(bf16[768,768]{1,0:T(8,128)(2,1)} %param.6) | copy-start | bytes 3538948
  49.2 2.6 %copy-start.3 = (bf16[768,768]{1,0:T(8,128)(2,1)S(1)}, bf16[768,768]{1,0:T(8,128)(2,1)}, u32[]{:S(2)}) copy-start(bf16[768,768]{1,0:T(8,128)(2,1)} %param.5) | copy-start | bytes 3538948
  49.2 4.3 %collective-permute-start = (bf16[256,1536]{1,0:T(8,128)(2,1)S(1)}, bf16[256,1536]{1,0:T(8,128)(2,1)S(1)}, u32[]{:S(2)}, u32[]{:S(2)}) collective-permute-start(bf16[256,1536]{1,0:T(8,128)(2,1)S(1)} %bitcast.17), channel_id=1, source_target_pairs={{0,1},{1,0},{2,3},{3,2},{4,5},{5,4},{6,7},{7,6},{8,9},{9,8},{10,11... | collective-permute-start | bytes 2359304 | tf_op jit(solution)/shard_map/ppermute | solution.py:31
  53.5 1.0 copy-start.5
  70.6 15.6 %all-to-all-start.3 = ((bf16[8,32,1536]{2,1,0:T(8,128)(2,1)}), bf16[8,32,1536]{2,1,0:T(8,128)(2,1)S(1)}, u32[]{:S(2)}, u32[]{:S(2)}) async-start(bf16[8,32,1536]{2,1,0:T(8,128)(2,1)} %bitcast.1), calls=%async_computation.3 | async-start | bytes 1572864 | tf_op jit(solution)/shard_map/all_to_all | solution.py:19
  77.5 10.4 %collective-permute-start.1 = (bf16[32,1536]{1,0:T(8,128)(2,1)}, bf16[32,1536]{1,0:T(8,128)(2,1)S(1)}, u32[]{:S(2)}, u32[]{:S(2)}) collective-permute-start(bf16[32,1536]{1,0:T(8,128)(2,1)} %reduce_sum.48), channel_id=1, source_target_pairs={{0,256},{256,0},{1,257},{257,1},{2,258},{258,2},{3,259},{259,3},{4... | collective-permute-start | bytes 294920 | tf_op jit(solution)/shard_map/ppermute | solution.py:31
  89.8 16.1 %all-to-all-start.4 = ((bf16[8,32,1536]{2,1,0:T(8,128)(2,1)}), bf16[8,32,1536]{2,1,0:T(8,128)(2,1)S(1)}, u32[]{:S(2)}, u32[]{:S(2)}) async-start(bf16[8,32,1536]{2,1,0:T(8,128)(2,1)} %broadcast_in_dim.10), calls=%async_computation.4 | async-start | bytes 1572864 | tf_op jit(solution)/shard_map/all_to_all | solution.py:19
  95.6 10.2 %collective-permute-start.2 = (bf16[32,1536]{1,0:T(8,128)(2,1)S(1)}, bf16[32,1536]{1,0:T(8,128)(2,1)S(1)}, u32[]{:S(2)}, u32[]{:S(2)}) collective-permute-start(bf16[32,1536]{1,0:T(8,128)(2,1)S(1)} %reduce_sum.49), channel_id=1, source_target_pairs={{0,256},{256,0},{1,257},{257,1},{2,258},{258,2},{3,259},{259,3},{4... | collective-permute-start | bytes 294920 | tf_op jit(solution)/shard_map/ppermute | solution.py:31
  106.8 13.2 %all-to-all-start.5 = ((bf16[8,32,1536]{2,1,0:T(8,128)(2,1)}), bf16[8,32,1536]{2,1,0:T(8,128)(2,1)S(1)}, u32[]{:S(2)}, u32[]{:S(2)}) async-start(bf16[8,32,1536]{2,1,0:T(8,128)(2,1)} %broadcast_in_dim.11), calls=%async_computation.5 | async-start | bytes 1572864 | tf_op jit(solution)/shard_map/all_to_all | solution.py:19
  114.9 4.3 %collective-permute-start.3 = (bf16[256,1536]{1,0:T(8,128)(2,1)S(1)}, bf16[256,1536]{1,0:T(8,128)(2,1)}, u32[]{:S(2)}, u32[]{:S(2)}) collective-permute-start(bf16[256,1536]{1,0:T(8,128)(2,1)S(1)} %pad_maximum_fusion.6), channel_id=1, source_target_pairs={{0,1},{1,0},{2,3},{3,2},{4,5},{5,4},{6,7},{7,6},{8,9},{9,8},{10,11... | collective-permute-start | bytes 2359304 | tf_op jit(solution)/shard_map/ppermute | solution.py:31
  120.1 1.8 %copy-start.1 = (bf16[8,32,1536]{2,1,0:T(8,128)(2,1)}, bf16[8,32,1536]{2,1,0:T(8,128)(2,1)S(1)}, u32[]{:S(2)}) copy-start(bf16[8,32,1536]{2,1,0:T(8,128)(2,1)S(1)} %all-to-all-done.5) | copy-start | bytes 2359300
  120.1 1.8 %copy-start.4 = (bf16[768,768]{1,0:T(8,128)(2,1)S(1)}, bf16[768,768]{1,0:T(8,128)(2,1)}, u32[]{:S(2)}) copy-start(bf16[768,768]{1,0:T(8,128)(2,1)} %param.5) | copy-start | bytes 3538948
  138.7 19.6 %all-to-all-start.7 = ((bf16[4,16,1536]{2,1,0:T(8,128)(2,1)}), bf16[4,16,1536]{2,1,0:T(8,128)(2,1)S(1)}, u32[]{:S(2)}, u32[]{:S(2)}) async-start(bf16[4,16,1536]{2,1,0:T(8,128)(2,1)} %bitcast.6), calls=%async_computation.7 | async-start | bytes 393216 | tf_op jit(solution)/shard_map/all_to_all | solution.py:19
  142.1 3.1 %copy-start.2 = (bf16[8,32,1536]{2,1,0:T(8,128)(2,1)S(1)}, bf16[8,32,1536]{2,1,0:T(8,128)(2,1)}, u32[]{:S(2)}) copy-start(bf16[8,32,1536]{2,1,0:T(8,128)(2,1)} %copy-done.1) | copy-start | bytes 2359300
  142.1 3.1 %copy-start.6 = (bf16[256,1536]{1,0:T(8,128)(2,1)S(1)}, bf16[256,1536]{1,0:T(8,128)(2,1)}, u32[]{:S(2)}) copy-start(bf16[256,1536]{1,0:T(8,128)(2,1)} %copy-done.5) | copy-start | bytes 2359300
